TPU v7x, 512 devices: a whole 4x8x8 slice. The times are simulated.
512 devices in a mesh: step: 8 (over x, core), row: 64 (over z, y).
Axes of the slice: x: 4, y: 8, z: 8, core: 2. Of those that a mesh axis runs over, the one named last changes fastest.
Arguments:
- trajectory: float32 [8, 4, 256, 128], P('step', None, 'row')
- noise: float32 [8, 4, 256, 128], P('step', None, 'row'), may hold values from -6 to 6
- tsteps: int32 [8, 2], P('step'), may hold values from 847 to 900, as said below
- w_in: bfloat16 [3, 3, 320, 4], replicated, may hold values from -1 to 1
- w_one: bfloat16 [3, 3, 320, 320], replicated, may hold values from -0.109375 to 0.109375
- w_two: bfloat16 [3, 3, 320, 320], replicated, may hold values from -0.109375 to 0.109375
- w_out: bfloat16 [3, 3, 4, 320], replicated, may hold values from -0.109375 to 0.109375
- w_time1: bfloat16 [320, 1280], replicated, may hold values from -0.3125 to 0.3125
- w_time2: bfloat16 [1280, 1280], replicated, may hold values from -0.15625 to 0.15625
- w_tproj: bfloat16 [1280, 320], replicated, may hold values from -0.15625 to 0.15625
Outputs:
- advanced: float32 [8, 4, 256, 128], P('step', None, 'row')
- slot_error: float32 [8], P('step')
Inputs may be any that keep to these rules, and one draw needn't show every extreme that they name: tsteps[0, 0] is 900; tsteps[i, 0] = 900 - 6 i - j with j of 0 to 5 for i > 0, and j = 5 for the last slot; tsteps[i, 1] = tsteps[i + 1, 0], and tsteps[i, 0] - 6 for the last slot.
All inputs are finite; a program needn't handle non-finite values.
Results may differ from a plain program's by a relative error of at most 0.0003.
Values may be sent and summed in bfloat16 or wider, within the bound.
A program may use at most 64 MiB of HBM per device.

v0:
```python
import math

import jax
import jax.numpy as jnp
from jax import lax
from jax.sharding import PartitionSpec as P

LATENT = 4
GROUPS = 32


noise_share = 0.5
norm_eps = 1e-05


def extended(cells, sides, width):
    for axis, dim in sides:
        count = lax.axis_size(axis)
        ends = count - 1
        head = lax.slice_in_dim(cells, 0, width, axis=dim)
        tail = lax.slice_in_dim(cells, cells.shape[dim] - width, cells.shape[dim], axis=dim)
        cells = jnp.concatenate(
            [
                lax.ppermute(tail, axis, [(i, (i + 1) % count) for i in range(ends)]),
                cells,
                lax.ppermute(head, axis, [((i + 1) % count, i) for i in range(ends)]),
            ],
            axis=dim,
        )
    return cells


def prefix(part, axis, combine, identity):
    place = lax.axis_index(axis)
    gathered = lax.all_gather(part, axis)
    state = jnp.zeros_like(part) + jnp.asarray(identity, part.dtype)

    def one(turn, state):
        return combine(state, lax.dynamic_index_in_dim(gathered, turn, 0, False))

    return lax.fori_loop(0, place, one, state)


def alpha_bar(level):
    angle = (level.astype(jnp.float32) / 1000.0 + 0.008) / 1.008 * (math.pi / 2)
    return jnp.cos(angle) ** 2


def conv_taps(padded, weight):
    channels, rows_in, width = padded.shape
    rows = rows_in - 2
    outputs = weight.shape[2]
    wide = jnp.pad(padded, ((0, 0), (0, 0), (1, 1)))
    total = jnp.zeros((outputs, rows * width), jnp.float32)
    for row_off in range(3):
        band = wide[:, row_off : row_off + rows]
        stacked = jnp.concatenate(
            [band[:, :, col_off : col_off + width] for col_off in range(3)], axis=0
        )
        stacked = stacked.reshape(3 * channels, rows * width)
        merged = jnp.transpose(weight[row_off], (1, 0, 2)).reshape(outputs, 3 * channels)
        total = total + jnp.dot(merged, stacked, preferred_element_type=jnp.float32)
    return total.reshape(outputs, rows, width)


def time_vector(level, w_time1, w_time2, w_tproj):
    half = w_time1.shape[0] // 2
    freq = jnp.exp(-math.log(10000.0) * jnp.arange(half, dtype=jnp.float32) / half)
    angle = level.astype(jnp.float32) * freq
    embed = jnp.concatenate([jnp.cos(angle), jnp.sin(angle)]).astype(jnp.bfloat16)
    hidden = jax.nn.silu(jnp.dot(embed, w_time1, preferred_element_type=jnp.float32)).astype(
        jnp.bfloat16
    )
    second = jax.nn.silu(jnp.dot(hidden, w_time2, preferred_element_type=jnp.float32)).astype(
        jnp.bfloat16
    )
    return jnp.dot(second, w_tproj, preferred_element_type=jnp.float32)


def group_norm(feature):
    channels, total_rows, width = feature.shape
    central = feature.reshape(GROUPS, -1)
    sums = jnp.sum(central, axis=1)
    squares = jnp.sum(central * central, axis=1)
    sums, squares = lax.psum((sums, squares), "row")
    count = central.shape[1] * lax.axis_size("row")
    mean = sums / count
    scale = lax.rsqrt(squares / count - mean * mean + norm_eps)
    grouped = feature.reshape(GROUPS, channels // GROUPS, total_rows, width)
    shifted = (grouped - mean[:, None, None, None]) * scale[:, None, None, None]
    return shifted.reshape(channels, total_rows, width)


def feature_conv(act, weight):
    padded = extended(act, (("row", 1),), 1)
    return conv_taps(padded, weight)


def add_terms(earlier, later):
    return earlier + later


def slot_drift(state, fresh, level, level_next, weights):
    w_in, w_one, w_two, w_out, w_time1, w_time2, w_tproj = weights
    tvec = time_vector(level, w_time1, w_time2, w_tproj)
    state_bf = state.astype(jnp.bfloat16)
    padded = extended(state_bf, (("row", 1),), 1)
    first = conv_taps(padded, w_in)
    act = jax.nn.silu(group_norm(first)).astype(jnp.bfloat16)
    second = feature_conv(act, w_one) + tvec[:, None, None]
    act = jax.nn.silu(group_norm(second)).astype(jnp.bfloat16)
    joined = first + feature_conv(act, w_two)
    act = jax.nn.silu(group_norm(joined)).astype(jnp.bfloat16)
    predicted = feature_conv(act, w_out)
    now = alpha_bar(level)
    after = alpha_bar(level_next)
    sigma = noise_share * jnp.sqrt((1.0 - after) / (1.0 - now) * (1.0 - now / after))
    keep_x = jnp.sqrt(after / now)
    keep_e = jnp.sqrt(1.0 - after - sigma * sigma) - jnp.sqrt(after) * jnp.sqrt(
        1.0 - now
    ) / jnp.sqrt(now)
    return keep_x * state + keep_e * predicted + sigma * fresh - state


def shards(trajectory, noise, tsteps, w_in, w_one, w_two, w_out, w_time1, w_time2, w_tproj):
    weights = (w_in, w_one, w_two, w_out, w_time1, w_time2, w_tproj)
    rows = trajectory.shape[2]
    width = trajectory.shape[3]
    height = rows * lax.axis_size("row")
    drifts = [slot_drift(trajectory[0], noise[0], tsteps[0, 0], tsteps[0, 1], weights)]
    step_index = lax.axis_index("step")
    leading = jnp.where(step_index == 0, trajectory[0], 0.0)
    terms = jnp.stack(drifts).at[0].add(leading)
    inclusive = jnp.cumsum(terms, axis=0)
    before = prefix(inclusive, "step", add_terms, jnp.zeros_like(inclusive))
    advanced = before + inclusive
    earlier = advanced - terms
    earlier = earlier.at[0].add(leading)
    local = jnp.sum((earlier - trajectory) ** 2, axis=(1, 2, 3))
    summed = lax.psum(local, "row")
    error = summed / (LATENT * height * width)
    return (advanced, error)


def solution(mesh):
    in_specs = (
        P("step", None, "row", None),
        P("step", None, "row", None),
        P("step", None),
        P(),
        P(),
        P(),
        P(),
        P(),
        P(),
        P(),
    )
    out_specs = (P("step", None, "row", None), P("step"))
    return jax.shard_map(shards, mesh=mesh, in_specs=in_specs, out_specs=out_specs, check_vma=False)
```

profile of v0, /device:TPU:6, one launch (start us, length us, event | category | flops | bytes accessed | tf_op | source)
XLA Modules:
  0.0 707.6 jit_solution(10656694157454589063)
XLA Ops:
  0.6 0.9 convert_bitcast_fusion
  1.5 3.6 collective-permute-start
  5.1 1.3 collective-permute-start.1
  6.4 0.7 slice_bitcast_fusion.9
  7.2 3.1 slice_bitcast_fusion.3
  10.3 0.6 fusion.74
  11.7 0.2 convolution_reduce_fusion.1
  12.0 0.5 convolution_reduce_fusion
  12.6 2.3 copy.21
  14.9 2.3 copy.22
  17.2 2.3 copy.23
  19.8 0.3 fusion.75
  20.1 0.3 convolution_add_fusion.1
  20.4 1.1 multiply_reduce_fusion.2
  21.5 1.2 reduce_sum.81
  23.2 151.0 %all-reduce.6 = (f32[32]{0:T(128)S(1)}, f32[32]{0:T(128)S(1)}) all-reduce(f32[32]{0:T(128)S(1)} %reduce_sum.89, f32[32]{0:T(128)S(1)} %reduce_sum.83), channel_id=1, replica_groups=mesh['step'=8,'row'=64] {'row'}, use_global_device_ids=true, to_apply=%region_5.6 | all-reduce | flops 64 | bytes 512 | tf_op jit(solution)/shard_map/psum | solution.py:85
  174.6 2.1 reshape.267
  176.7 2.3 fusion.48
  179.2 1.3 collective-permute-start.2
  180.5 1.5 collective-permute-start.3
  182.0 1.5 convolution_reduce_fusion.2
  183.5 4.3 collective-permute-done.3
  187.8 1.7 fusion.10
  189.5 1.2 fusion.68
  190.6 9.8 %fusion.45 = (bf16[960,4,128]{2,1,0:T(4,128)(2,1)S(1)}, bf16[960,4,128]{2,1,0:T(4,128)(2,1)S(1)}, bf16[960,4,128]{2,1,0:T(4,128)(2,1)S(1)}) fusion(bf16[320,1,128]{2,1,0:T(2,128)(2,1)S(1)} %collective-permute-done.3, bf16[320,4,128]{2,1,0:T(4,128)(2,1)S(1)} %fusion.48, bf16[320,4,128]{2,1,0:T(4,128)(2,1)S(1)} %get-tuple-element.93, ...), kind=kLoop, calls=%fused_computation.66 | loop fusion | flops 10813440 | bytes 5406720 | tf_op jit(solution)/shard_map/concatenate | solution.py:57
  200.5 0.6 fusion.33
  201.0 0.5 copy-done.6
  201.5 0.6 convolution_add_fusion.5
  202.2 1.4 add_reduce_fusion
  204.0 138.0 %all-reduce.5 = (f32[32]{0:T(128)S(1)}, f32[32]{0:T(128)S(1)}) all-reduce(f32[32]{0:T(128)S(1)} %reduce_sum.118, f32[32]{0:T(128)S(1)} %reduce_sum.92), channel_id=1, replica_groups=mesh['step'=8,'row'=64] {'row'}, use_global_device_ids=true, to_apply=%region_11.12 | all-reduce | flops 64 | bytes 512 | tf_op jit(solution)/shard_map/psum | solution.py:85
  342.4 2.2 reshape.274
  344.5 2.9 fusion.49
  347.5 0.7 copy-done.4
  348.2 1.0 fusion.70
  349.2 3.9 collective-permute-start.4
  353.1 1.5 collective-permute-start.5
  354.6 3.0 slice_bitcast_fusion
  357.6 2.3 copy.24
  359.9 2.3 copy.25
  362.2 2.3 copy.26
  364.5 2.8 fusion.8
  367.3 1.2 fusion.67
  368.5 9.8 %fusion.41 = (bf16[960,4,128]{2,1,0:T(4,128)(2,1)S(1)}, bf16[960,4,128]{2,1,0:T(4,128)(2,1)S(1)}, bf16[960,4,128]{2,1,0:T(4,128)(2,1)S(1)}) fusion(bf16[320,1,128]{2,1,0:T(2,128)(2,1)} %collective-permute-done.5, bf16[320,4,128]{2,1,0:T(4,128)(2,1)S(1)} %copy-done.5, bf16[320,4,128]{2,1,0:T(4,128)(2,1)S(1)} %get-tuple-element.87, ...), kind=kLoop, calls=%fused_computation.60 | loop fusion | flops 10813440 | bytes 5406720 | tf_op jit(solution)/shard_map/concatenate | solution.py:57
  378.3 0.6 fusion.26
  378.8 0.5 copy-done.8
  379.4 0.6 convolution_add_fusion.3
  380.2 1.4 add_reduce_fusion.1
  382.1 141.0 %all-reduce.4 = (f32[32]{0:T(128)S(1)}, f32[32]{0:T(128)S(1)}) all-reduce(f32[32]{0:T(128)S(1)} %reduce_sum.124, f32[32]{0:T(128)S(1)} %reduce_sum.121), channel_id=1, replica_groups=mesh['step'=8,'row'=64] {'row'}, use_global_device_ids=true, to_apply=%region_17.18 | all-reduce | flops 64 | bytes 512 | tf_op jit(solution)/shard_map/psum | solution.py:85
  523.5 2.1 reshape.281
  525.6 2.4 fusion.50
  528.0 0.7 copy-done.2
  528.7 0.9 fusion.69
  529.7 1.3 collective-permute-start.6
  531.0 1.6 collective-permute-start.7
  534.1 4.4 collective-permute-done.7
  538.5 2.8 select_maximum_fusion
  541.3 1.2 fusion.66
  542.5 9.8 %fusion.37 = (bf16[960,4,128]{2,1,0:T(4,128)(2,1)S(1)}, bf16[960,4,128]{2,1,0:T(4,128)(2,1)S(1)}, bf16[960,4,128]{2,1,0:T(4,128)(2,1)S(1)}) fusion(bf16[320,1,128]{2,1,0:T(2,128)(2,1)} %collective-permute-done.7, bf16[320,4,128]{2,1,0:T(4,128)(2,1)S(1)} %copy-done.3, bf16[320,4,128]{2,1,0:T(4,128)(2,1)S(1)} %get-tuple-element.81, ...), kind=kLoop, calls=%fused_computation.54 | loop fusion | flops 10813440 | bytes 5406720 | tf_op jit(solution)/shard_map/concatenate | solution.py:57
  552.3 0.2 fusion.19
  552.5 0.2 convolution_add_fusion.7
  552.8 0.2 fusion.14
  553.1 12.8 %all_gather.4 = f32[8,1,4,4,128]{4,3,2,1,0:T(4,128)S(1)} all-gather(f32[1,1,4,4,128]{4,3,2,1,0:T(4,128)S(1)} %fusion.62), channel_id=1, replica_groups=mesh['step'=8,'row'=64] {'step'}, dimensions={0}, use_global_device_ids=true | all-gather | bytes 73728 | tf_op jit(solution)/shard_map/all_gather | solution.py:35
  566.1 1.2 multiply_reduce_fusion.3
  567.3 138.6 %psum.55 = f32[1]{0:T(128)} all-reduce(f32[1]{0:T(128)} %bitcast.40), channel_id=1, replica_groups=mesh['step'=8,'row'=64] {'row'}, use_global_device_ids=true, to_apply=%region_21.22 | all-reduce | flops 1 | bytes 8 | tf_op jit(solution)/shard_map/psum | solution.py:140
  (102 shorter events, 4.2 us)
Async XLA Ops:
  0.6 11.3 %copy-start = (bf16[1280,1280]{1,0:T(8,128)(2,1)S(1)}, bf16[1280,1280]{1,0:T(8,128)(2,1)}, u32[]{:S(2)}) copy-start(bf16[1280,1280]{1,0:T(8,128)(2,1)} %param.24) | copy-start | bytes 9830404
  1.5 18.0 %collective-permute-start = (bf16[4,1,128]{2,1,0:T(2,128)(2,1)S(1)}, bf16[4,1,128]{2,1,0:T(2,128)(2,1)S(1)}, u32[]{:S(2)}, u32[]{:S(2)}) collective-permute-start(bf16[4,1,128]{2,1,0:T(2,128)(2,1)S(1)} %get-tuple-element.125), channel_id=1, source_target_pairs={{0,1},{1,2},{2,3},{3,4},{4,5},{5,6},{6,7},{7,8},{8,9},{9,10},{10,1... | collective-permute-start | bytes 3080 | tf_op jit(solution)/shard_map/ppermute | solution.py:24
  5.1 14.4 %collective-permute-start.1 = (bf16[4,1,128]{2,1,0:T(2,128)(2,1)S(1)}, bf16[4,1,128]{2,1,0:T(2,128)(2,1)S(1)}, u32[]{:S(2)}, u32[]{:S(2)}) collective-permute-start(bf16[4,1,128]{2,1,0:T(2,128)(2,1)S(1)} %get-tuple-element.124), channel_id=1, source_target_pairs={{1,0},{2,1},{3,2},{4,3},{5,4},{6,5},{7,6},{8,7},{9,8},{10,9},{11,1... | collective-permute-start | bytes 3080 | tf_op jit(solution)/shard_map/ppermute | solution.py:26
  7.2 3.1 copy-start.16
  7.2 4.5 copy-start.9
  179.2 4.3 collective-permute-start.2
  180.5 7.3 %collective-permute-start.3 = (bf16[320,1,128]{2,1,0:T(2,128)(2,1)S(1)}, bf16[320,1,128]{2,1,0:T(2,128)(2,1)S(1)}, u32[]{:S(2)}, u32[]{:S(2)}) collective-permute-start(bf16[320,1,128]{2,1,0:T(2,128)(2,1)S(1)} %get-tuple-element.107), channel_id=1, source_target_pairs={{1,0},{2,1},{3,2},{4,3},{5,4},{6,5},{7,6},{8,7},{9,8},{10,9},{11,1... | collective-permute-start | bytes 245768 | tf_op jit(solution)/shard_map/ppermute | solution.py:26
  190.6 9.8 %copy-start.11 = (bf16[320,3,320]{0,2,1:T(8,128)(2,1)S(1)}, bf16[320,3,320]{0,2,1:T(8,128)(2,1)}, u32[]{:S(2)}) copy-start(bf16[320,3,320]{0,2,1:T(8,128)(2,1)} %copy.21) | copy-start | bytes 1843204
  200.4 1.1 copy-start.6
  201.0 1.2 copy-start.10
  347.5 0.7 copy-start.4
  349.2 15.3 %collective-permute-start.4 = (bf16[320,1,128]{2,1,0:T(2,128)(2,1)}, bf16[320,1,128]{2,1,0:T(2,128)(2,1)S(1)}, u32[]{:S(2)}, u32[]{:S(2)}) collective-permute-start(bf16[320,1,128]{2,1,0:T(2,128)(2,1)} %get-tuple-element.103), channel_id=1, source_target_pairs={{0,1},{1,2},{2,3},{3,4},{4,5},{5,6},{6,7},{7,8},{8,9},{9,10},{10,1... | collective-permute-start | bytes 245768 | tf_op jit(solution)/shard_map/ppermute | solution.py:24
  353.1 11.4 %collective-permute-start.5 = (bf16[320,1,128]{2,1,0:T(2,128)(2,1)}, bf16[320,1,128]{2,1,0:T(2,128)(2,1)}, u32[]{:S(2)}, u32[]{:S(2)}) collective-permute-start(bf16[320,1,128]{2,1,0:T(2,128)(2,1)} %get-tuple-element.102), channel_id=1, source_target_pairs={{1,0},{2,1},{3,2},{4,3},{5,4},{6,5},{7,6},{8,7},{9,8},{10,9},{11,1... | collective-permute-start | bytes 245768 | tf_op jit(solution)/shard_map/ppermute | solution.py:26
  367.3 1.2 copy-start.5
  368.5 9.8 %copy-start.12 = (bf16[320,3,320]{0,2,1:T(8,128)(2,1)S(1)}, bf16[320,3,320]{0,2,1:T(8,128)(2,1)}, u32[]{:S(2)}) copy-start(bf16[320,3,320]{0,2,1:T(8,128)(2,1)} %copy.24) | copy-start | bytes 1843204
  378.2 1.1 copy-start.8
  378.8 1.1 copy-start.1
  378.8 1.4 copy-start.7
  381.6 150.9 %copy-start.15 = (bf16[3,3,4,320]{3,2,1,0:T(4,128)(2,1)S(1)}, bf16[3,3,4,320]{3,2,1,0:T(4,128)(2,1)}, u32[]{:S(2)}) copy-start(bf16[3,3,4,320]{3,2,1,0:T(4,128)(2,1)} %param.22) | copy-start | bytes 69124
  528.0 0.7 copy-start.2
  529.7 4.4 collective-permute-start.6
  531.0 7.5 %collective-permute-start.7 = (bf16[320,1,128]{2,1,0:T(2,128)(2,1)}, bf16[320,1,128]{2,1,0:T(2,128)(2,1)}, u32[]{:S(2)}, u32[]{:S(2)}) collective-permute-start(bf16[320,1,128]{2,1,0:T(2,128)(2,1)} %get-tuple-element.97), channel_id=1, source_target_pairs={{1,0},{2,1},{3,2},{4,3},{5,4},{6,5},{7,6},{8,7},{9,8},{10,9},{11,1... | collective-permute-start | bytes 245768 | tf_op jit(solution)/shard_map/ppermute | solution.py:26
  541.3 1.2 copy-start.3
  552.2 0.8 copy-start.13
  552.3 0.8 copy-start.14
where the time goes:
time: 720 us; the launch traced here: 708 us
  blocking collectives  581 us (81%)
  other arithmetic  48.6 us (7%)
  local copies, waits for them, and re-layouts  38.3 us (5%)
  starting transfers between devices  15.9 us (2%)
  matrix products  9.77 us (1%)
  waiting for transfers between devices  8.69 us (1%)
    psum x3, blocking collectives, group_norm(): sums, squares = lax.psum((sums, squares), 'row')  430 us
    psum x1, blocking collectives, shards(): summed = lax.psum(local, 'row')  139 us
    concatenate x4, other arithmetic, conv_taps(): jnp.concatenate([band[:, :, col_off:col_off + width] for col_off in range...  29.3 us
    transpose x13, local copies, waits for them, and re-layouts, conv_taps(): jnp.transpose(weight[row_off], (1, 0, 2)).reshape(outputs, 3 * channels)  20.6 us
  transfers between devices with their start and end apart: 8, of which 2 were waited for; matrix products, arithmetic and copies ran while one was open for 3% of the time, Pallas kernels for 0%

commit v1 on v0

v1 whole, which is shorter than its diff:
```python
import functools
import math

import jax
import jax.numpy as jnp
from jax import lax
from jax.experimental import pallas as pl
from jax.experimental.pallas import tpu as pltpu
from jax.sharding import PartitionSpec as P

MESH = pl.DeviceIdType.MESH
F32 = jnp.float32
BF16 = jnp.bfloat16
LATENT = 4
GROUPS = 32
LANES = 128
ROWS = 4
NORM_EPS = 1e-05
NOISE_SHARE = 0.5


def dot(a, b):
    return jnp.dot(a, b, preferred_element_type=F32)


def offsets(nz, ny):
    hops = lambda d, n: min(d, n - d)
    every = [(dz, dy) for dz in range(nz) for dy in range(ny) if (dz, dy) != (0, 0)]
    return sorted(every, key=lambda o: -(hops(o[0], nz) + hops(o[1], ny)))


def silu(x):
    return x / (1.0 + jnp.exp(-x))


def shifted(x, col):
    if col == 1:
        return x
    lane = lax.broadcasted_iota(jnp.int32, x.shape, x.ndim - 1)
    if col == 0:
        return jnp.where(lane == 0, 0.0, pltpu.roll(x, 1, axis=x.ndim - 1))
    return jnp.where(lane == LANES - 1, 0.0, pltpu.roll(x, LANES - 1, axis=x.ndim - 1))


def kernel(
    nz, ny, nsteps, channels, temb, height,
    traj_h, noise_h, ts_h, w_in_h, w_one_h, w_two_h, w_out_h, wt1_h, wt2_h, wtp_h,
    adv_ref, err_ref,
    traj, noise, ts, w_in, w_one, w_two, w_out, wt1, wt2, wtp,
    win_f, win_m, wone_m, wtwo_m, wout_f,
    xbuf, xcol, h0, h1, rr, acts, vt, mcol, scol, tcol,
    msg, sums, terms, tbuf,
    load_sem, x_send, x_recv, h_send, h_recv, ar_send, ar_recv, t_send, t_recv,
):
    nrow = nz * ny
    row = lax.axis_index("row")
    step = lax.axis_index("step")
    mz, my = row // ny, lax.rem(row, ny)
    peers = [
        lax.rem(mz + dz, nz) * ny + lax.rem(my + dy, ny) for dz, dy in offsets(nz, ny)
    ]
    others = [lax.rem(step + d, nsteps) for d in range(1, nsteps)]
    below = lax.rem(row + 1, nrow)
    above = lax.rem(row + nrow - 1, nrow)
    per_group = channels // GROUPS

    barrier = pltpu.get_barrier_semaphore()
    for p in peers:
        pl.semaphore_signal(barrier, inc=1, device_id={"row": p}, device_id_type=MESH)
    for s in others:
        pl.semaphore_signal(barrier, inc=1, device_id={"step": s}, device_id_type=MESH)

    loads = [
        (traj_h, traj), (noise_h, noise), (ts_h, ts), (w_in_h, w_in), (w_one_h, w_one),
        (wt1_h, wt1), (wt2_h, wt2), (wtp_h, wtp), (w_two_h, w_two), (w_out_h, w_out),
    ]
    copies = [
        pltpu.make_async_copy(src, dst, load_sem.at[i]) for i, (src, dst) in enumerate(loads)
    ]
    for c in copies:
        c.start()
    (c_traj, c_noise, c_ts, c_win, c_wone, c_wt1, c_wt2, c_wtp, c_wtwo, c_wout) = copies

    c_traj.wait()
    for r in range(ROWS):
        xbuf[2 + r] = traj[0, :, r, :]

    xcol[...] = jnp.zeros_like(xcol)
    win_f[...] = jnp.zeros_like(win_f)
    c_win.wait()
    for p in range(3):
        for q in range(3):
            tap = 4 * (3 * p + q)
            win_f[tap : tap + 4, :channels] = w_in[p, q].astype(F32)
    win_m[...] = jnp.transpose(win_f[...])[:channels].astype(BF16)

    pl.semaphore_wait(barrier, nrow - 1 + nsteps - 1)

    up = pltpu.make_async_remote_copy(
        xbuf.at[pl.ds(2, 2)], xbuf.at[pl.ds(6, 2)], x_send.at[0], x_recv.at[0],
        device_id={"row": above}, device_id_type=MESH,
    )
    down = pltpu.make_async_remote_copy(
        xbuf.at[pl.ds(4, 2)], xbuf.at[pl.ds(0, 2)], x_send.at[1], x_recv.at[1],
        device_id={"row": below}, device_id_type=MESH,
    )
    up.start()
    down.start()

    def merge(weights, merged):
        for q in range(3):
            merged[q] = jnp.concatenate([weights[p, q] for p in range(3)], axis=1)

    c_wone.wait()
    merge(w_one, wone_m)

    is_top = row == 0
    is_bottom = row == nrow - 1

    def send_sums(k, line):
        msg[k] = line
        sums[k, pl.ds(row, 1), :] = line
        for p in peers:
            pltpu.make_async_remote_copy(
                msg.at[k], sums.at[k, pl.ds(row, 1), :], ar_send.at[k], ar_recv.at[k],
                device_id={"row": p}, device_id_type=MESH,
            ).start()

    def others_of(k):
        return sums.at[k, pl.ds(0, nrow - 1), :]

    def total_sums(k):
        part = others_of(k)
        pltpu.make_async_copy(part, part, ar_recv.at[k]).wait()
        return jnp.sum(sums[k], axis=0, keepdims=True)

    group_of = lax.broadcasted_iota(jnp.int32, (GROUPS, channels), 0) * per_group
    channel = lax.broadcasted_iota(jnp.int32, (GROUPS, channels), 1)
    members = jnp.where(
        (channel >= group_of) & (channel < group_of + per_group), 1.0, 0.0
    ).astype(BF16)

    def group_line(rows):
        total = functools.reduce(lambda a, b: a + b, rows)
        square = functools.reduce(lambda a, b: a + b, [v * v for v in rows])
        both = jnp.concatenate([total, square], axis=1)
        high = both.astype(BF16)
        rest = both - high.astype(F32)
        mid = rest.astype(BF16)
        low = (rest - mid.astype(F32)).astype(BF16)
        grouped = dot(members, high) + dot(members, mid) + dot(members, low)
        stacked = jnp.concatenate(
            [grouped[:, :LANES], grouped[:, LANES:], jnp.zeros((64, LANES), F32)], axis=0
        )
        return jnp.sum(jnp.transpose(stacked), axis=0, keepdims=True)

    count = per_group * height * LANES

    def norm_columns(k):
        total = total_sums(k) * (1.0 / count)
        lane = lax.broadcasted_iota(jnp.int32, total.shape, 1)
        square = pltpu.roll(total, LANES - GROUPS, axis=1)
        variance = jnp.where(lane < GROUPS, square - total * total, 1.0)
        scale = lax.rsqrt(variance + NORM_EPS)
        line = jnp.where(lane < GROUPS, total, pltpu.roll(scale, GROUPS, axis=1))
        vt[...] = jnp.transpose(jnp.broadcast_to(line, (LANES, LANES)))
        sub = lax.broadcasted_iota(jnp.int32, (8, LANES), 0)
        for first, target in ((0, mcol), (GROUPS, scol)):
            for j in range(channels // 8):
                low, high = 8 * j // per_group, (8 * j + 7) // per_group
                value = jnp.broadcast_to(vt[first + low : first + low + 1, :], (8, LANES))
                if high != low:
                    other = jnp.broadcast_to(vt[first + high : first + high + 1, :], (8, LANES))
                    value = jnp.where(sub < high * per_group - 8 * j, value, other)
                target[8 * j : 8 * j + 8, :] = value

    def activate(source, r):
        act = silu((source[r] - mcol[...]) * scol[...])
        if r == 0:
            act = jnp.where(is_top, 0.0, act)
        if r == ROWS + 1:
            act = jnp.where(is_bottom, 0.0, act)
        return act.astype(BF16)

    def place(r, act):
        for p in range(3):
            if 0 <= r - p < ROWS:
                acts[p * channels : (p + 1) * channels, (r - p) * LANES : (r - p + 1) * LANES] = act

    def conv(merged, source, finish):
        for r in range(ROWS + 2):
            place(r, activate(source, r))
        for half in range(ROWS // 2):
            x = acts[:, half * 2 * LANES : (half + 1) * 2 * LANES]
            y = [dot(merged[q], x) for q in range(3)]
            for i in range(2):
                cut = slice(i * LANES, (i + 1) * LANES)
                finish(2 * half + i, sum(shifted(y[q][:, cut], q) for q in range(3)))

    def halo_copies(buf, k):
        return [
            pltpu.make_async_remote_copy(
                buf.at[1], buf.at[ROWS + 1], h_send.at[k, 0], h_recv.at[k, 0],
                device_id={"row": above}, device_id_type=MESH,
            ),
            pltpu.make_async_remote_copy(
                buf.at[ROWS], buf.at[0], h_send.at[k, 1], h_recv.at[k, 1],
                device_id={"row": below}, device_id_type=MESH,
            ),
        ]

    up.wait_recv()
    down.wait_recv()
    for r in range(ROWS + 4):
        x = xbuf[r]
        if r < 2:
            x = jnp.where(is_top, 0.0, x)
        if r >= ROWS + 2:
            x = jnp.where(is_bottom, 0.0, x)
        for q in range(3):
            moved = shifted(x, q)
            for p in range(3):
                if 0 <= r - p < ROWS + 2:
                    tap = 4 * (3 * p + q)
                    xcol[tap : tap + 4, (r - p) * LANES : (r - p + 1) * LANES] = moved
    first = dot(win_m[:, :48], xcol[...].astype(BF16))
    for r in range(ROWS + 2):
        h0[r] = first[:, r * LANES : (r + 1) * LANES]
    send_sums(0, group_line([h0[r] for r in range(1, ROWS + 1)]))

    c_ts.wait()
    times = ts[...].astype(F32)
    level = jnp.broadcast_to(times[:, 0:1], (1, LANES))
    level_next = jnp.broadcast_to(times[:, 1:2], (1, LANES))
    c_wt1.wait()
    half = channels // 2
    lane = lax.broadcasted_iota(jnp.int32, (LANES, channels), 1)
    place_of = jnp.where(lane < half, lane, lane - half).astype(F32)
    freq = jnp.exp(-math.log(10000.0) * place_of / half)
    angle = jnp.broadcast_to(times[:, 0:1], (LANES, channels)) * freq
    embed = jnp.where(lane < half, jnp.cos(angle), jnp.sin(angle)).astype(BF16)
    hidden = silu(dot(embed, wt1[...])).astype(BF16)
    c_wt2.wait()
    second = silu(dot(hidden, wt2[...])).astype(BF16)
    c_wtp.wait()
    tcol[...] = lax.dot_general(
        wtp[...], second, (((1,), (1,)), ((), ())), preferred_element_type=F32
    )

    c_wtwo.wait()
    merge(w_two, wtwo_m)
    c_wout.wait()
    wout_f[...] = jnp.zeros_like(wout_f)
    for p in range(3):
        for q in range(3):
            tap = 8 * (3 * p + q)
            wout_f[tap : tap + 4, :] = w_out[p, q].astype(F32)

    def alpha_bar(t):
        return jnp.cos((t / 1000.0 + 0.008) / 1.008 * (math.pi / 2)) ** 2

    now, after = alpha_bar(level), alpha_bar(level_next)
    sigma = NOISE_SHARE * jnp.sqrt((1.0 - after) / (1.0 - now) * (1.0 - now / after))
    keep_x = jnp.sqrt(after / now)
    keep_e = jnp.sqrt(1.0 - after - sigma * sigma) - jnp.sqrt(after) * jnp.sqrt(
        1.0 - now
    ) / jnp.sqrt(now)

    norm_columns(0)

    def finish_one(r, value):
        h1[1 + r] = value + tcol[...]

    conv(wone_m, h0, finish_one)
    halo1 = halo_copies(h1, 0)
    for c in halo1:
        c.start()
    send_sums(1, group_line([h1[r] for r in range(1, ROWS + 1)]))

    norm_columns(1)
    for c in halo1:
        c.wait_recv()

    def finish_two(r, value):
        rr[1 + r] = value + h0[1 + r]

    conv(wtwo_m, h1, finish_two)
    halo2 = halo_copies(rr, 1)
    for c in halo2:
        c.start()
    send_sums(2, group_line([rr[r] for r in range(1, ROWS + 1)]))

    c_noise.wait()
    norm_columns(2)
    for c in halo2:
        c.wait_recv()
    a3 = jnp.concatenate([activate(rr, r) for r in range(ROWS + 2)], axis=1)
    y = dot(wout_f[...].astype(BF16), a3)
    is_first = step == 0
    for r in range(ROWS):
        eps = jnp.zeros((8, LANES), F32)
        for q in range(3):
            column = jnp.zeros((8, LANES), F32)
            for p in range(3):
                tap = 8 * (3 * p + q)
                column += y[tap : tap + 8, (r + p) * LANES : (r + p + 1) * LANES]
            eps += shifted(column, q)
        x = traj[0, :, r, :]
        term = keep_x * x + keep_e * eps[:LATENT] + sigma * noise[0, :, r, :] - x
        term = term + jnp.where(is_first, x, 0.0)
        tbuf[r] = term
        terms[step, r] = term

    for s in others:
        pltpu.make_async_remote_copy(
            tbuf, terms.at[step], t_send, t_recv, device_id={"step": s}, device_id_type=MESH,
        ).start()
    came = terms.at[pl.ds(0, nsteps - 1)]
    pltpu.make_async_copy(came, came, t_recv).wait()
    error = jnp.zeros((LATENT, LANES), F32)
    for r in range(ROWS):
        earlier = jnp.zeros((LATENT, LANES), F32)
        for s in range(nsteps - 1):
            earlier = earlier + jnp.where(s < step, terms[s, r], 0.0)
        adv_ref[0, :, r, :] = earlier + tbuf[r]
        x = traj[0, :, r, :]
        gap = jnp.where(is_first, 0.0, earlier - x)
        error = error + gap * gap
    send_sums(3, jnp.sum(error, axis=0, keepdims=True))
    err_ref[0] = jnp.sum(total_sums(3)) * (1.0 / (LATENT * height * LANES))

    up.wait_send()
    down.wait_send()
    for c in halo1 + halo2:
        c.wait_send()
    for k in range(4):
        part = others_of(k)
        pltpu.make_async_copy(part, part, ar_send.at[k]).wait()
    pltpu.make_async_copy(came, came, t_send).wait()


def shards(nz, ny, nsteps, trajectory, noise, tsteps, w_in, w_one, w_two, w_out, wt1, wt2, wtp):
    w_in = jnp.transpose(w_in, (0, 1, 3, 2))
    wtp = jnp.transpose(wtp)
    args = (trajectory, noise, tsteps, w_in, w_one, w_two, w_out, wt1, wt2, wtp)
    channels, temb = wt1.shape
    nrow = nz * ny
    height = trajectory.shape[2] * nrow
    vmem = lambda shape, dtype: pltpu.VMEM(shape, dtype)
    scratch = [vmem(a.shape, a.dtype) for a in args] + [
        vmem((LANES, -(-channels // LANES) * LANES), F32),
        vmem((channels, LANES), BF16),
        vmem((3, channels, 3 * channels), BF16),
        vmem((3, channels, 3 * channels), BF16),
        vmem((80, channels), F32),
        vmem((ROWS + 4, LATENT, LANES), F32),
        vmem((48, (ROWS + 2) * LANES), F32),
        vmem((ROWS + 2, channels, LANES), F32),
        vmem((ROWS + 2, channels, LANES), F32),
        vmem((ROWS + 2, channels, LANES), F32),
        vmem((3 * channels, ROWS * LANES), BF16),
        vmem((LANES, LANES), F32),
        vmem((channels, LANES), F32),
        vmem((channels, LANES), F32),
        vmem((channels, LANES), F32),
        vmem((4, 1, LANES), F32),
        vmem((4, nrow, LANES), F32),
        vmem((nsteps, ROWS, LATENT, LANES), F32),
        vmem((ROWS, LATENT, LANES), F32),
        pltpu.SemaphoreType.DMA((len(args),)),
        pltpu.SemaphoreType.DMA((2,)),
        pltpu.SemaphoreType.DMA((2,)),
        pltpu.SemaphoreType.DMA((2, 2)),
        pltpu.SemaphoreType.DMA((2, 2)),
        pltpu.SemaphoreType.DMA((4,)),
        pltpu.SemaphoreType.DMA((4,)),
        pltpu.SemaphoreType.DMA,
        pltpu.SemaphoreType.DMA,
    ]
    return pl.pallas_call(
        functools.partial(kernel, nz, ny, nsteps, channels, temb, height),
        out_shape=(
            jax.ShapeDtypeStruct(trajectory.shape, F32),
            jax.ShapeDtypeStruct((1,), F32),
        ),
        in_specs=[pl.BlockSpec(memory_space=pltpu.HBM)] * len(args),
        out_specs=(
            pl.BlockSpec(memory_space=pltpu.VMEM),
            pl.BlockSpec(memory_space=pltpu.SMEM),
        ),
        scratch_shapes=scratch,
        compiler_params=pltpu.CompilerParams(
            collective_id=0, has_side_effects=True, vmem_limit_bytes=56 * 1024 * 1024
        ),
    )(*args)


def solution(mesh):
    nsteps, nrow = mesh.shape["step"], mesh.shape["row"]
    ny = 8 if nrow % 8 == 0 else 2
    place = P("step", None, "row", None)
    return jax.shard_map(
        functools.partial(shards, nrow // ny, ny, nsteps),
        mesh=mesh,
        in_specs=(place, place, P("step", None)) + (P(),) * 7,
        out_specs=(place, P("step")),
        check_vma=False,
    )
```

time: 720 us -> 64.4 us (0.09)
  the two profiles are of different devices: /device:TPU:6 before, /device:TPU:1 now
where the time goes in v1:
time: 64.4 us; the launch traced here: 64.2 us
  Pallas kernels  60.5 us (94%)
  between operations  2.41 us (4%)
  local copies, waits for them, and re-layouts  1.3 us (2%)
    pallas_call x1, Pallas kernels, shards(): pl.pallas_call(functools.partial(kernel, nz, ny, nsteps, channels, temb,...  60.5 us
    unnamed x1, local copies, waits for them, and re-layouts  1.3 us

profile of v1, /device:TPU:1, one launch (start us, length us, event | category | flops | bytes accessed | tf_op | source)
XLA Modules:
  0.0 64.2 jit_solution(1430552217457689563)
XLA Ops:
  0.6 60.5 %shard_map.113 = (f32[1,4,4,128]{3,2,1,0:T(4,128)}, f32[1]{0:T(128)}) custom-call(f32[1,4,4,128]{3,2,1,0:T(4,128)} %traj_h.1, f32[1,4,4,128]{3,2,1,0:T(4,128)} %noise_h.1, s32[1,2]{1,0:T(1,128)} %ts_h.1, bf16[3,3,4,320]{3,2,1,0:T(4,128)(2,1)} %bitcast.3, bf16[3,3,320,320]{3,2,1,0:T(8,128)(2,1)} %w_one_h.1, bf16[3,3,320,320]{3,2,1,0:T(8,128)(2,1)} %w_two_h.1, ...), custom_call_target="tpu_custom_call" | custom-call | tf_op jit(solution)/shard_map/pallas_call | solution.py:380
  61.1 1.3 %copy.14 = f32[1,4,4,128]{3,2,1,0:T(4,128)} copy(f32[1,4,4,128]{3,2,1,0:T(4,128)} %get-tuple-element.4) | data formatting | bytes 16384

commit v2 on v1

--- a/solution.py
+++ b/solution.py
@@ -30,7 +30,8 @@
 
 
 def silu(x):
-    return x / (1.0 + jnp.exp(-x))
+    half = 0.5 * x
+    return half + half * jnp.tanh(half)
 
 
 def shifted(x, col):
@@ -50,7 +51,7 @@
     win_f, win_m, wone_m, wtwo_m, wout_f,
     xbuf, xcol, h0, h1, rr, acts, vt, mcol, scol, tcol,
     msg, sums, terms, tbuf,
-    load_sem, x_send, x_recv, h_send, h_recv, ar_send, ar_recv, t_send, t_recv,
+    load_sem, x_send, x_recv, h_send, h_recv, ar_send, ar_recv, t_send, t_recv, line_sem, adv, err, out_sem,
 ):
     nrow = nz * ny
     row = lax.axis_index("row")
@@ -64,8 +65,10 @@
     above = lax.rem(row + nrow - 1, nrow)
     per_group = channels // GROUPS
 
+    column = [lax.rem(mz + d, nz) * ny + my for d in range(1, nz)]
+    line = [mz * ny + lax.rem(my + d, ny) for d in range(1, ny)]
     barrier = pltpu.get_barrier_semaphore()
-    for p in peers:
+    for p in column + line + [above, below]:
         pl.semaphore_signal(barrier, inc=1, device_id={"row": p}, device_id_type=MESH)
     for s in others:
         pl.semaphore_signal(barrier, inc=1, device_id={"step": s}, device_id_type=MESH)
@@ -94,7 +97,7 @@
             win_f[tap : tap + 4, :channels] = w_in[p, q].astype(F32)
     win_m[...] = jnp.transpose(win_f[...])[:channels].astype(BF16)
 
-    pl.semaphore_wait(barrier, nrow - 1 + nsteps - 1)
+    pl.semaphore_wait(barrier, nz - 1 + ny - 1 + 2 + nsteps - 1)
 
     up = pltpu.make_async_remote_copy(
         xbuf.at[pl.ds(2, 2)], xbuf.at[pl.ds(6, 2)], x_send.at[0], x_recv.at[0],
@@ -106,6 +109,8 @@
     )
     up.start()
     down.start()
+    for p in column:
+        pl.semaphore_signal(line_sem, inc=1, device_id={"row": p}, device_id_type=MESH)
 
     def merge(weights, merged):
         for q in range(3):
@@ -226,6 +231,7 @@
     first = dot(win_m[:, :48], xcol[...].astype(BF16))
     for r in range(ROWS + 2):
         h0[r] = first[:, r * LANES : (r + 1) * LANES]
+    pl.semaphore_wait(line_sem, nz - 1)
     send_sums(0, group_line([h0[r] for r in range(1, ROWS + 1)]))
 
     c_ts.wait()
@@ -273,9 +279,9 @@
 
     conv(wone_m, h0, finish_one)
     halo1 = halo_copies(h1, 0)
+    send_sums(1, group_line([h1[r] for r in range(1, ROWS + 1)]))
     for c in halo1:
         c.start()
-    send_sums(1, group_line([h1[r] for r in range(1, ROWS + 1)]))
 
     norm_columns(1)
     for c in halo1:
@@ -286,9 +292,9 @@
 
     conv(wtwo_m, h1, finish_two)
     halo2 = halo_copies(rr, 1)
+    send_sums(2, group_line([rr[r] for r in range(1, ROWS + 1)]))
     for c in halo2:
         c.start()
-    send_sums(2, group_line([rr[r] for r in range(1, ROWS + 1)]))
 
     c_noise.wait()
     norm_columns(2)
@@ -322,12 +328,17 @@
         earlier = jnp.zeros((LATENT, LANES), F32)
         for s in range(nsteps - 1):
             earlier = earlier + jnp.where(s < step, terms[s, r], 0.0)
-        adv_ref[0, :, r, :] = earlier + tbuf[r]
+        adv[0, :, r, :] = earlier + tbuf[r]
         x = traj[0, :, r, :]
         gap = jnp.where(is_first, 0.0, earlier - x)
         error = error + gap * gap
+    adv_out = pltpu.make_async_copy(adv, adv_ref, out_sem.at[0])
+    adv_out.start()
     send_sums(3, jnp.sum(error, axis=0, keepdims=True))
-    err_ref[0] = jnp.sum(total_sums(3)) * (1.0 / (LATENT * height * LANES))
+    whole = jnp.sum(total_sums(3), axis=1, keepdims=True)
+    err[...] = whole * (1.0 / (LATENT * height * LANES))
+    err_out = pltpu.make_async_copy(err, err_ref, out_sem.at[1])
+    err_out.start()
 
     up.wait_send()
     down.wait_send()
@@ -337,6 +348,26 @@
         part = others_of(k)
         pltpu.make_async_copy(part, part, ar_send.at[k]).wait()
     pltpu.make_async_copy(came, came, t_send).wait()
+    adv_out.wait()
+    err_out.wait()
+
+
+def finish(advanced, error, advanced_out, error_out, adv, err, sem):
+    come = [
+        pltpu.make_async_copy(advanced, adv, sem.at[0]),
+        pltpu.make_async_copy(error, err, sem.at[1]),
+    ]
+    go = [
+        pltpu.make_async_copy(adv, advanced_out, sem.at[2]),
+        pltpu.make_async_copy(err, error_out, sem.at[3]),
+    ]
+    for c in come:
+        c.start()
+    for c, g in zip(come, go):
+        c.wait()
+        g.start()
+    for g in go:
+        g.wait()
 
 
 def shards(nz, ny, nsteps, trajectory, noise, tsteps, w_in, w_one, w_two, w_out, wt1, wt2, wtp):
@@ -376,28 +407,47 @@
         pltpu.SemaphoreType.DMA((4,)),
         pltpu.SemaphoreType.DMA,
         pltpu.SemaphoreType.DMA,
-    ]
-    return pl.pallas_call(
+        pltpu.SemaphoreType.REGULAR,
+        vmem(trajectory.shape, F32),
+        vmem((1, 1), F32),
+        pltpu.SemaphoreType.DMA((2,)),
+    ]
+    advanced, error = pl.pallas_call(
         functools.partial(kernel, nz, ny, nsteps, channels, temb, height),
         out_shape=(
             jax.ShapeDtypeStruct(trajectory.shape, F32),
-            jax.ShapeDtypeStruct((1,), F32),
+            jax.ShapeDtypeStruct((1, 1), F32),
         ),
         in_specs=[pl.BlockSpec(memory_space=pltpu.HBM)] * len(args),
-        out_specs=(
-            pl.BlockSpec(memory_space=pltpu.VMEM),
-            pl.BlockSpec(memory_space=pltpu.SMEM),
-        ),
+        out_specs=(pl.BlockSpec(memory_space=pltpu.HBM),) * 2,
         scratch_shapes=scratch,
         compiler_params=pltpu.CompilerParams(
             collective_id=0, has_side_effects=True, vmem_limit_bytes=56 * 1024 * 1024
         ),
     )(*args)
+    advanced, error = pl.pallas_call(
+        finish,
+        out_shape=(
+            jax.ShapeDtypeStruct(trajectory.shape, F32),
+            jax.ShapeDtypeStruct((1, 1), F32),
+        ),
+        in_specs=[pl.BlockSpec(memory_space=pltpu.HBM)] * 2,
+        out_specs=(
+            pl.BlockSpec(memory_space=pltpu.HBM),
+            pl.BlockSpec(memory_space=pltpu.HBM),
+        ),
+        scratch_shapes=[
+            pltpu.VMEM(trajectory.shape, F32),
+            pltpu.VMEM((1, 1), F32),
+            pltpu.SemaphoreType.DMA((4,)),
+        ],
+    )(advanced, error)
+    return advanced, error.reshape(1)
 
 
 def solution(mesh):
     nsteps, nrow = mesh.shape["step"], mesh.shape["row"]
-    ny = 8 if nrow % 8 == 0 else 2
+    ny = 8 if nrow % 8 == 0 else min(2, nrow)
     place = P("step", None, "row", None)
     return jax.shard_map(
         functools.partial(shards, nrow // ny, ny, nsteps),

time: 64.4 us -> 59.3 us (0.921)
  Pallas kernels: 60.5 us -> 58.4 us
  between operations: 2.41 us -> 0.64 us
  local copies, waits for them, and re-layouts: 1.3 us -> 0 us
    pallas_call x1, Pallas kernels: 60.5 us -> 56.5 us  [shards(): pl.pallas_call(functools.partial(kernel, nz, ny, nsteps, channels, temb,...]
    pallas_call x0 -> x1, Pallas kernels: none -> 1.96 us  [shards(): pl.pallas_call(finish, out_shape=(jax.ShapeDtypeStruct(trajectory.shape,...]
    unnamed x1 -> x0, local copies, waits for them, and re-layouts: 1.3 us -> none
where the time goes in v2:
time: 59.3 us; the launch traced here: 59.1 us
  Pallas kernels  58.4 us (98%)
  between operations  0.64 us (1%)
    pallas_call x1, Pallas kernels, shards(): pl.pallas_call(functools.partial(kernel, nz, ny, nsteps, channels, temb,...  56.5 us
    pallas_call x1, Pallas kernels, shards(): pl.pallas_call(finish, out_shape=(jax.ShapeDtypeStruct(trajectory.shape,...  1.96 us

profile of v2, /device:TPU:1, one launch (start us, length us, event | category | flops | bytes accessed | tf_op | source)
XLA Modules:
  0.0 59.1 jit_solution(6594965732680593727)
XLA Ops:
  0.6 56.5 %shard_map.113 = (f32[1,4,4,128]{3,2,1,0:T(4,128)}, f32[1,1]{1,0:T(1,128)}) custom-call(f32[1,4,4,128]{3,2,1,0:T(4,128)} %traj_h.1, f32[1,4,4,128]{3,2,1,0:T(4,128)} %noise_h.1, s32[1,2]{1,0:T(1,128)} %ts_h.1, bf16[3,3,4,320]{3,2,1,0:T(4,128)(2,1)} %bitcast.4, bf16[3,3,320,320]{3,2,1,0:T(8,128)(2,1)} %w_one_h.1, bf16[3,3,320,320]{3,2,1,0:T(8,128)(2,1)} %w_two_h.1, ...), custom_call_target="tpu_custom_call" | custom-call | tf_op jit(solution)/shard_map/pallas_call | solution.py:415
  57.1 2.0 %shard_map.114 = (f32[1,4,4,128]{3,2,1,0:T(4,128)}, f32[1,1]{1,0:T(1,128)}) custom-call(f32[1,4,4,128]{3,2,1,0:T(4,128)} %get-tuple-element.6.advanced, f32[1,1]{1,0:T(1,128)} %get-tuple-element.7.error), custom_call_target="tpu_custom_call" | custom-call | tf_op jit(solution)/shard_map/pallas_call | solution.py:428

commit v3 on v1

--- a/solution.py
+++ b/solution.py
@@ -30,7 +30,8 @@
 
 
 def silu(x):
-    return x / (1.0 + jnp.exp(-x))
+    half = 0.5 * x
+    return half + half * jnp.tanh(half)
 
 
 def shifted(x, col):
@@ -45,12 +46,12 @@
 def kernel(
     nz, ny, nsteps, channels, temb, height,
     traj_h, noise_h, ts_h, w_in_h, w_one_h, w_two_h, w_out_h, wt1_h, wt2_h, wtp_h,
-    adv_ref, err_ref,
+    out_ref,
     traj, noise, ts, w_in, w_one, w_two, w_out, wt1, wt2, wtp,
     win_f, win_m, wone_m, wtwo_m, wout_f,
     xbuf, xcol, h0, h1, rr, acts, vt, mcol, scol, tcol,
     msg, sums, terms, tbuf,
-    load_sem, x_send, x_recv, h_send, h_recv, ar_send, ar_recv, t_send, t_recv,
+    load_sem, x_send, x_recv, h_send, h_recv, ar_send, ar_recv, t_send, t_recv, line_sem,
 ):
     nrow = nz * ny
     row = lax.axis_index("row")
@@ -64,8 +65,12 @@
     above = lax.rem(row + nrow - 1, nrow)
     per_group = channels // GROUPS
 
+    terms[...] = jnp.zeros_like(terms)
+
+    column = [lax.rem(mz + d, nz) * ny + my for d in range(1, nz)]
+    line = [mz * ny + lax.rem(my + d, ny) for d in range(1, ny)]
     barrier = pltpu.get_barrier_semaphore()
-    for p in peers:
+    for p in column + line + [above, below]:
         pl.semaphore_signal(barrier, inc=1, device_id={"row": p}, device_id_type=MESH)
     for s in others:
         pl.semaphore_signal(barrier, inc=1, device_id={"step": s}, device_id_type=MESH)
@@ -94,7 +99,7 @@
             win_f[tap : tap + 4, :channels] = w_in[p, q].astype(F32)
     win_m[...] = jnp.transpose(win_f[...])[:channels].astype(BF16)
 
-    pl.semaphore_wait(barrier, nrow - 1 + nsteps - 1)
+    pl.semaphore_wait(barrier, nz - 1 + ny - 1 + 2 + nsteps - 1)
 
     up = pltpu.make_async_remote_copy(
         xbuf.at[pl.ds(2, 2)], xbuf.at[pl.ds(6, 2)], x_send.at[0], x_recv.at[0],
@@ -106,6 +111,8 @@
     )
     up.start()
     down.start()
+    for p in column:
+        pl.semaphore_signal(line_sem, inc=1, device_id={"row": p}, device_id_type=MESH)
 
     def merge(weights, merged):
         for q in range(3):
@@ -143,27 +150,31 @@
     def group_line(rows):
         total = functools.reduce(lambda a, b: a + b, rows)
         square = functools.reduce(lambda a, b: a + b, [v * v for v in rows])
-        both = jnp.concatenate([total, square], axis=1)
+        lane = lax.broadcasted_iota(jnp.int32, total.shape, 1)
+        both = jnp.where(
+            lane < LANES // 2,
+            total + pltpu.roll(total, LANES // 2, axis=1),
+            square + pltpu.roll(square, LANES // 2, axis=1),
+        )
         high = both.astype(BF16)
         rest = both - high.astype(F32)
         mid = rest.astype(BF16)
         low = (rest - mid.astype(F32)).astype(BF16)
-        grouped = dot(members, high) + dot(members, mid) + dot(members, low)
+        grouped = dot(members, jnp.concatenate([high, mid, low], axis=1))
+        grouped = grouped[:, :LANES] + grouped[:, LANES : 2 * LANES] + grouped[:, 2 * LANES :]
         stacked = jnp.concatenate(
-            [grouped[:, :LANES], grouped[:, LANES:], jnp.zeros((64, LANES), F32)], axis=0
+            [grouped, pltpu.roll(grouped, LANES // 2, axis=1), jnp.zeros((64, LANES), F32)], axis=0
         )
-        return jnp.sum(jnp.transpose(stacked), axis=0, keepdims=True)
+        return jnp.sum(jnp.transpose(stacked)[: LANES // 2], axis=0, keepdims=True)
 
     count = per_group * height * LANES
 
     def norm_columns(k):
         total = total_sums(k) * (1.0 / count)
-        lane = lax.broadcasted_iota(jnp.int32, total.shape, 1)
-        square = pltpu.roll(total, LANES - GROUPS, axis=1)
-        variance = jnp.where(lane < GROUPS, square - total * total, 1.0)
-        scale = lax.rsqrt(variance + NORM_EPS)
-        line = jnp.where(lane < GROUPS, total, pltpu.roll(scale, GROUPS, axis=1))
-        vt[...] = jnp.transpose(jnp.broadcast_to(line, (LANES, LANES)))
+        columns = jnp.transpose(jnp.broadcast_to(total, (LANES, LANES)))
+        mean, square = columns[:GROUPS], columns[GROUPS : 2 * GROUPS]
+        vt[:GROUPS, :] = mean
+        vt[GROUPS:, :] = 0.5 * lax.rsqrt(square - mean * mean + NORM_EPS)
         sub = lax.broadcasted_iota(jnp.int32, (8, LANES), 0)
         for first, target in ((0, mcol), (GROUPS, scol)):
             for j in range(channels // 8):
@@ -175,7 +186,8 @@
                 target[8 * j : 8 * j + 8, :] = value
 
     def activate(source, r):
-        act = silu((source[r] - mcol[...]) * scol[...])
+        half = (source[r] - mcol[...]) * scol[...]
+        act = half + half * jnp.tanh(half)
         if r == 0:
             act = jnp.where(is_top, 0.0, act)
         if r == ROWS + 1:
@@ -188,9 +200,9 @@
                 acts[p * channels : (p + 1) * channels, (r - p) * LANES : (r - p + 1) * LANES] = act
 
     def conv(merged, source, finish):
-        for r in range(ROWS + 2):
-            place(r, activate(source, r))
         for half in range(ROWS // 2):
+            for r in range(ROWS) if half == 0 else (ROWS, ROWS + 1):
+                place(r, activate(source, r))
             x = acts[:, half * 2 * LANES : (half + 1) * 2 * LANES]
             y = [dot(merged[q], x) for q in range(3)]
             for i in range(2):
@@ -226,6 +238,7 @@
     first = dot(win_m[:, :48], xcol[...].astype(BF16))
     for r in range(ROWS + 2):
         h0[r] = first[:, r * LANES : (r + 1) * LANES]
+    pl.semaphore_wait(line_sem, nz - 1)
     send_sums(0, group_line([h0[r] for r in range(1, ROWS + 1)]))
 
     c_ts.wait()
@@ -273,9 +286,9 @@
 
     conv(wone_m, h0, finish_one)
     halo1 = halo_copies(h1, 0)
+    send_sums(1, group_line([h1[r] for r in range(1, ROWS + 1)]))
     for c in halo1:
         c.start()
-    send_sums(1, group_line([h1[r] for r in range(1, ROWS + 1)]))
 
     norm_columns(1)
     for c in halo1:
@@ -286,9 +299,9 @@
 
     conv(wtwo_m, h1, finish_two)
     halo2 = halo_copies(rr, 1)
+    send_sums(2, group_line([rr[r] for r in range(1, ROWS + 1)]))
     for c in halo2:
         c.start()
-    send_sums(2, group_line([rr[r] for r in range(1, ROWS + 1)]))
 
     c_noise.wait()
     norm_columns(2)
@@ -309,25 +322,35 @@
         term = keep_x * x + keep_e * eps[:LATENT] + sigma * noise[0, :, r, :] - x
         term = term + jnp.where(is_first, x, 0.0)
         tbuf[r] = term
-        terms[step, r] = term
-
-    for s in others:
-        pltpu.make_async_remote_copy(
-            tbuf, terms.at[step], t_send, t_recv, device_id={"step": s}, device_id_type=MESH,
-        ).start()
-    came = terms.at[pl.ds(0, nsteps - 1)]
-    pltpu.make_async_copy(came, came, t_recv).wait()
+
+    def to_later(d):
+        return pltpu.make_async_remote_copy(
+            tbuf, terms.at[step], t_send.at[d - 1], t_recv.at[step],
+            device_id={"step": lax.rem(step + d, nsteps)}, device_id_type=MESH,
+        )
+
+    for d in range(1, nsteps):
+        @pl.when(step + d < nsteps)
+        def _():
+            to_later(d).start()
+    for s in range(nsteps - 1):
+        @pl.when(s < step)
+        def _():
+            pltpu.make_async_copy(tbuf, tbuf, t_recv.at[s]).wait()
     error = jnp.zeros((LATENT, LANES), F32)
     for r in range(ROWS):
         earlier = jnp.zeros((LATENT, LANES), F32)
         for s in range(nsteps - 1):
-            earlier = earlier + jnp.where(s < step, terms[s, r], 0.0)
-        adv_ref[0, :, r, :] = earlier + tbuf[r]
+            earlier = earlier + terms[s, r]
+        out_ref[0, :LATENT, r, :] = earlier + tbuf[r]
         x = traj[0, :, r, :]
         gap = jnp.where(is_first, 0.0, earlier - x)
         error = error + gap * gap
     send_sums(3, jnp.sum(error, axis=0, keepdims=True))
-    err_ref[0] = jnp.sum(total_sums(3)) * (1.0 / (LATENT * height * LANES))
+    whole = jnp.sum(total_sums(3), axis=1, keepdims=True)
+    out_ref[0, LATENT] = jnp.broadcast_to(
+        whole * (1.0 / (LATENT * height * LANES)), (ROWS, LANES)
+    )
 
     up.wait_send()
     down.wait_send()
@@ -336,7 +359,22 @@
     for k in range(4):
         part = others_of(k)
         pltpu.make_async_copy(part, part, ar_send.at[k]).wait()
-    pltpu.make_async_copy(came, came, t_send).wait()
+    for d in range(1, nsteps):
+        @pl.when(step + d < nsteps)
+        def _():
+            to_later(d).wait_send()
+
+
+def finish(both, advanced_out, error_out, error, sem):
+    copies = [
+        pltpu.make_async_copy(both.at[:, pl.ds(0, LATENT)], advanced_out, sem.at[0]),
+        pltpu.make_async_copy(error, error_out, sem.at[1]),
+    ]
+    copies[0].start()
+    error[...] = both[0, LATENT, 0:1, 0:1]
+    copies[1].start()
+    for c in copies:
+        c.wait()
 
 
 def shards(nz, ny, nsteps, trajectory, noise, tsteps, w_in, w_one, w_two, w_out, wt1, wt2, wtp):
@@ -359,13 +397,13 @@
         vmem((ROWS + 2, channels, LANES), F32),
         vmem((ROWS + 2, channels, LANES), F32),
         vmem((3 * channels, ROWS * LANES), BF16),
-        vmem((LANES, LANES), F32),
+        vmem((2 * GROUPS, LANES), F32),
         vmem((channels, LANES), F32),
         vmem((channels, LANES), F32),
         vmem((channels, LANES), F32),
         vmem((4, 1, LANES), F32),
         vmem((4, nrow, LANES), F32),
-        vmem((nsteps, ROWS, LATENT, LANES), F32),
+        vmem((nsteps - 1, ROWS, LATENT, LANES), F32),
         vmem((ROWS, LATENT, LANES), F32),
         pltpu.SemaphoreType.DMA((len(args),)),
         pltpu.SemaphoreType.DMA((2,)),
@@ -374,30 +412,36 @@
         pltpu.SemaphoreType.DMA((2, 2)),
         pltpu.SemaphoreType.DMA((4,)),
         pltpu.SemaphoreType.DMA((4,)),
-        pltpu.SemaphoreType.DMA,
-        pltpu.SemaphoreType.DMA,
+        pltpu.SemaphoreType.DMA((nsteps - 1,)),
+        pltpu.SemaphoreType.DMA((nsteps - 1,)),
+        pltpu.SemaphoreType.REGULAR,
     ]
-    return pl.pallas_call(
+    both = pl.pallas_call(
         functools.partial(kernel, nz, ny, nsteps, channels, temb, height),
-        out_shape=(
-            jax.ShapeDtypeStruct(trajectory.shape, F32),
-            jax.ShapeDtypeStruct((1,), F32),
-        ),
+        out_shape=pltpu.VMEM((1, LATENT + 1, ROWS, LANES), F32),
         in_specs=[pl.BlockSpec(memory_space=pltpu.HBM)] * len(args),
-        out_specs=(
-            pl.BlockSpec(memory_space=pltpu.VMEM),
-            pl.BlockSpec(memory_space=pltpu.SMEM),
-        ),
+        out_specs=pl.BlockSpec(memory_space=pltpu.VMEM),
         scratch_shapes=scratch,
         compiler_params=pltpu.CompilerParams(
             collective_id=0, has_side_effects=True, vmem_limit_bytes=56 * 1024 * 1024
         ),
     )(*args)
+    advanced, error = pl.pallas_call(
+        finish,
+        out_shape=(
+            jax.ShapeDtypeStruct(trajectory.shape, F32),
+            jax.ShapeDtypeStruct((1, 1), F32),
+        ),
+        in_specs=[pl.BlockSpec(memory_space=pltpu.VMEM)],
+        out_specs=(pl.BlockSpec(memory_space=pltpu.HBM),) * 2,
+        scratch_shapes=[pltpu.VMEM((1, 1), F32), pltpu.SemaphoreType.DMA((2,))],
+    )(pltpu.with_memory_space_constraint(both, pltpu.VMEM))
+    return advanced, error.reshape(1)
 
 
 def solution(mesh):
     nsteps, nrow = mesh.shape["step"], mesh.shape["row"]
-    ny = 8 if nrow % 8 == 0 else 2
+    ny = 8 if nrow % 8 == 0 else min(2, nrow)
     place = P("step", None, "row", None)
     return jax.shard_map(
         functools.partial(shards, nrow // ny, ny, nsteps),

time: 64.4 us -> 54.9 us (0.85)
  the two profiles are of different devices: /device:TPU:1 before, /device:TPU:6 now
where the time goes in v3:
time: 54.9 us; the launch traced here: 54.8 us
  Pallas kernels  54.1 us (99%)
  between operations  0.64 us (1%)
    pallas_call x1, Pallas kernels, shards(): pl.pallas_call(functools.partial(kernel, nz, ny, nsteps, channels, temb,...  53.5 us

profile of v3, /device:TPU:6, one launch (start us, length us, event | category | flops | bytes accessed | tf_op | source)
XLA Modules:
  0.0 54.8 jit_solution(17696959760537071521)
XLA Ops:
  0.6 53.5 %shard_map.113.both = f32[1,5,4,128]{3,2,1,0:T(4,128)S(1)} custom-call(f32[1,4,4,128]{3,2,1,0:T(4,128)} %traj_h.1, f32[1,4,4,128]{3,2,1,0:T(4,128)} %noise_h.1, s32[1,2]{1,0:T(1,128)} %ts_h.1, bf16[3,3,4,320]{3,2,1,0:T(4,128)(2,1)} %bitcast.4, bf16[3,3,320,320]{3,2,1,0:T(8,128)(2,1)} %w_one_h.1, bf16[3,3,320,320]{3,2,1,0:T(8,128)(2,1)} %w_two_h.1, ...), custom_call_target="tpu_custom_call" | custom-call | tf_op jit(solution)/shard_map/pallas_call | solution.py:419
  54.1 0.6 %shard_map.114 = (f32[1,4,4,128]{3,2,1,0:T(4,128)}, f32[1,1]{1,0:T(1,128)}) custom-call(f32[1,5,4,128]{3,2,1,0:T(4,128)S(1)} %shard_map.113.both), custom_call_target="tpu_custom_call" | custom-call | tf_op jit(solution)/shard_map/pallas_call | solution.py:429

commit v4 on v3

--- a/solution.py
+++ b/solution.py
@@ -51,7 +51,7 @@
     win_f, win_m, wone_m, wtwo_m, wout_f,
     xbuf, xcol, h0, h1, rr, acts, vt, mcol, scol, tcol,
     msg, sums, terms, tbuf,
-    load_sem, x_send, x_recv, h_send, h_recv, ar_send, ar_recv, t_send, t_recv, line_sem,
+    load_sem, x_send, x_recv, h_send, h_recv, ar_send, ar_recv, t_send, t_recv, line_sem, end_sem,
 ):
     nrow = nz * ny
     row = lax.axis_index("row")
@@ -67,11 +67,18 @@
 
     terms[...] = jnp.zeros_like(terms)
 
+    def at_end(y):
+        return (y == 0) | (y == ny - 1) if ny >= 4 else y < 0
+
     column = [lax.rem(mz + d, nz) * ny + my for d in range(1, nz)]
     line = [mz * ny + lax.rem(my + d, ny) for d in range(1, ny)]
     barrier = pltpu.get_barrier_semaphore()
-    for p in column + line + [above, below]:
+    for p in column + [above, below]:
         pl.semaphore_signal(barrier, inc=1, device_id={"row": p}, device_id_type=MESH)
+    for d, p in enumerate(line, 1):
+        @pl.when(jnp.logical_not(at_end(lax.rem(my + d, ny))))
+        def _():
+            pl.semaphore_signal(barrier, inc=1, device_id={"row": p}, device_id_type=MESH)
     for s in others:
         pl.semaphore_signal(barrier, inc=1, device_id={"step": s}, device_id_type=MESH)
 
@@ -99,7 +106,8 @@
             win_f[tap : tap + 4, :channels] = w_in[p, q].astype(F32)
     win_m[...] = jnp.transpose(win_f[...])[:channels].astype(BF16)
 
-    pl.semaphore_wait(barrier, nz - 1 + ny - 1 + 2 + nsteps - 1)
+    here = at_end(my)
+    pl.semaphore_wait(barrier, nz - 1 + 2 + nsteps - 1 + jnp.where(here, 0, ny - 1))
 
     up = pltpu.make_async_remote_copy(
         xbuf.at[pl.ds(2, 2)], xbuf.at[pl.ds(6, 2)], x_send.at[0], x_recv.at[0],
@@ -111,6 +119,18 @@
     )
     up.start()
     down.start()
+    if ny >= 4:
+        @pl.when((my == 1) | (my == ny - 2))
+        def _():
+            pl.semaphore_signal(
+                end_sem, inc=1, device_id={"row": jnp.where(my == 1, above, below)},
+                device_id_type=MESH,
+            )
+
+        @pl.when(here)
+        def _():
+            pl.semaphore_wait(end_sem, 1)
+
     for p in column:
         pl.semaphore_signal(line_sem, inc=1, device_id={"row": p}, device_id_type=MESH)
 
@@ -329,7 +349,7 @@
             device_id={"step": lax.rem(step + d, nsteps)}, device_id_type=MESH,
         )
 
-    for d in range(1, nsteps):
+    for d in range(nsteps - 1, 0, -1):
         @pl.when(step + d < nsteps)
         def _():
             to_later(d).start()
@@ -415,6 +435,7 @@
         pltpu.SemaphoreType.DMA((nsteps - 1,)),
         pltpu.SemaphoreType.DMA((nsteps - 1,)),
         pltpu.SemaphoreType.REGULAR,
+        pltpu.SemaphoreType.REGULAR,
     ]
     both = pl.pallas_call(
         functools.partial(kernel, nz, ny, nsteps, channels, temb, height),
@@ -441,7 +462,7 @@
 
 def solution(mesh):
     nsteps, nrow = mesh.shape["step"], mesh.shape["row"]
-    ny = 8 if nrow % 8 == 0 else min(2, nrow)
+    ny = 8 if nrow % 64 == 0 else max(1, nrow // 2)
     place = P("step", None, "row", None)
     return jax.shard_map(
         functools.partial(shards, nrow // ny, ny, nsteps),

time: 54.9 us -> 54.6 us (level)
  no operation moved by 1% of the time
where the time goes in v4:
time: 54.6 us; the launch traced here: 54.4 us
  Pallas kernels  53.7 us (98%)
  between operations  0.64 us (1%)
    pallas_call x1, Pallas kernels, shards(): pl.pallas_call(functools.partial(kernel, nz, ny, nsteps, channels, temb,...  53.1 us

profile of v4, /device:TPU:6, one launch (start us, length us, event | category | flops | bytes accessed | tf_op | source)
XLA Modules:
  0.0 54.4 jit_solution(15074447732684434753)
XLA Ops:
  0.6 53.1 %shard_map.113.both = f32[1,5,4,128]{3,2,1,0:T(4,128)S(1)} custom-call(f32[1,4,4,128]{3,2,1,0:T(4,128)} %traj_h.1, f32[1,4,4,128]{3,2,1,0:T(4,128)} %noise_h.1, s32[1,2]{1,0:T(1,128)} %ts_h.1, bf16[3,3,4,320]{3,2,1,0:T(4,128)(2,1)} %bitcast.4, bf16[3,3,320,320]{3,2,1,0:T(8,128)(2,1)} %w_one_h.1, bf16[3,3,320,320]{3,2,1,0:T(8,128)(2,1)} %w_two_h.1, ...), custom_call_target="tpu_custom_call" | custom-call | tf_op jit(solution)/shard_map/pallas_call | solution.py:440
  53.7 0.6 %shard_map.114 = (f32[1,4,4,128]{3,2,1,0:T(4,128)}, f32[1,1]{1,0:T(1,128)}) custom-call(f32[1,5,4,128]{3,2,1,0:T(4,128)S(1)} %shard_map.113.both), custom_call_target="tpu_custom_call" | custom-call | tf_op jit(solution)/shard_map/pallas_call | solution.py:450

commit v5 on v4

--- a/solution.py
+++ b/solution.py
@@ -258,8 +258,9 @@
     first = dot(win_m[:, :48], xcol[...].astype(BF16))
     for r in range(ROWS + 2):
         h0[r] = first[:, r * LANES : (r + 1) * LANES]
+    first_line = group_line([h0[r] for r in range(1, ROWS + 1)])
     pl.semaphore_wait(line_sem, nz - 1)
-    send_sums(0, group_line([h0[r] for r in range(1, ROWS + 1)]))
+    send_sums(0, first_line)
 
     c_ts.wait()
     times = ts[...].astype(F32)
@@ -367,22 +368,25 @@
         gap = jnp.where(is_first, 0.0, earlier - x)
         error = error + gap * gap
     send_sums(3, jnp.sum(error, axis=0, keepdims=True))
+    up.wait_send()
+    down.wait_send()
+    for c in halo1 + halo2:
+        c.wait_send()
+    for k in range(3):
+        part = others_of(k)
+        pltpu.make_async_copy(part, part, ar_send.at[k]).wait()
+    for d in range(1, nsteps):
+        @pl.when(step + d < nsteps)
+        def _():
+            to_later(d).wait_send()
+
     whole = jnp.sum(total_sums(3), axis=1, keepdims=True)
     out_ref[0, LATENT] = jnp.broadcast_to(
         whole * (1.0 / (LATENT * height * LANES)), (ROWS, LANES)
     )
 
-    up.wait_send()
-    down.wait_send()
-    for c in halo1 + halo2:
-        c.wait_send()
-    for k in range(4):
-        part = others_of(k)
-        pltpu.make_async_copy(part, part, ar_send.at[k]).wait()
-    for d in range(1, nsteps):
-        @pl.when(step + d < nsteps)
-        def _():
-            to_later(d).wait_send()
+    part = others_of(3)
+    pltpu.make_async_copy(part, part, ar_send.at[3]).wait()
 
 
 def finish(both, advanced_out, error_out, error, sem):

time: 54.6 us -> 54.5 us (level)
  no operation moved by 1% of the time
where the time goes in v5:
time: 54.5 us; the launch traced here: 54.3 us
  Pallas kernels  53.6 us (98%)
  between operations  0.64 us (1%)
    pallas_call x1, Pallas kernels, shards(): pl.pallas_call(functools.partial(kernel, nz, ny, nsteps, channels, temb,...  53 us

profile of v5, /device:TPU:6, one launch (start us, length us, event | category | flops | bytes accessed | tf_op | source)
XLA Modules:
  0.0 54.3 jit_solution(8714933810823445324)
XLA Ops:
  0.6 53.0 %shard_map.113.both = f32[1,5,4,128]{3,2,1,0:T(4,128)S(1)} custom-call(f32[1,4,4,128]{3,2,1,0:T(4,128)} %traj_h.1, f32[1,4,4,128]{3,2,1,0:T(4,128)} %noise_h.1, s32[1,2]{1,0:T(1,128)} %ts_h.1, bf16[3,3,4,320]{3,2,1,0:T(4,128)(2,1)} %bitcast.4, bf16[3,3,320,320]{3,2,1,0:T(8,128)(2,1)} %w_one_h.1, bf16[3,3,320,320]{3,2,1,0:T(8,128)(2,1)} %w_two_h.1, ...), custom_call_target="tpu_custom_call" | custom-call | tf_op jit(solution)/shard_map/pallas_call | solution.py:444
  53.6 0.6 %shard_map.114 = (f32[1,4,4,128]{3,2,1,0:T(4,128)}, f32[1,1]{1,0:T(1,128)}) custom-call(f32[1,5,4,128]{3,2,1,0:T(4,128)S(1)} %shard_map.113.both), custom_call_target="tpu_custom_call" | custom-call | tf_op jit(solution)/shard_map/pallas_call | solution.py:454
